TPU v7x, 128 devices: a whole 4x4x4 slice. The times are simulated.
128 devices in a mesh: dp: 8 (over z, y_hi), tensor: 16 (over x, y_lo, core).
Axes of the slice: x: 4, y: 4 (y_hi: 2, y_lo: 2; y = y_hi * 2 + y_lo), z: 4, core: 2. Of those that a mesh axis runs over, the one named last changes fastest.
Arguments:
- doc_rows: bfloat16 [1024, 8192], P('tensor', 'dp'), may hold values from -6 to 6
- packed_slot: int32 [1024], P('tensor'), may hold values from 0 to 1023, as said below
- gate_weight: bfloat16 [8192, 28672], P('dp', 'tensor'), may hold values from -0.0625 to 0.0625
- up_weight: bfloat16 [8192, 28672], P('dp', 'tensor'), may hold values from -0.0625 to 0.0625
- down_weight: bfloat16 [28672, 8192], P('tensor', 'dp'), may hold values from -0.03125 to 0.03125
Outputs:
- mixed: bfloat16 [1024, 8192], P('tensor', 'dp')
Inputs may be any that keep to these rules, and one draw needn't show every extreme that they name: packed_slot is a permutation of 0 to 1023. Call positions p with p // 64 equal a block. The rows of one index of tensor (aligned runs of 64 rows) put at most 8 rows into one block, and each such run puts exactly 8 rows into some block.
All inputs are finite; a program needn't handle non-finite values.
Results may differ from a plain program's by a relative error of at most 0.02.
Values may be sent and summed in bfloat16 or wider, within the bound.
A program may use at most 128 MiB of HBM per device.

v0:
```python
import jax
import jax.numpy as jnp
from jax import lax
from jax.sharding import PartitionSpec as P


def local(doc_rows, packed_slot, gate_weight, up_weight, down_weight):
    tensor_count = lax.axis_size("tensor")
    row_count = doc_rows.shape[0]
    slot_cap = row_count // 8
    width_part = doc_rows.shape[1]
    hidden_part = gate_weight.shape[1]
    target_block = packed_slot // row_count
    block_slot = packed_slot % row_count
    one_hot = (target_block[:, None] == jnp.arange(tensor_count, dtype=jnp.int32)[None, :]).astype(
        jnp.int32
    )
    earlier = jnp.cumsum(one_hot, axis=0) - one_hot
    send_rank = jnp.sum(earlier * one_hot, axis=1)
    flat_index = target_block * slot_cap + send_rank
    send_rows = (
        jnp.zeros((tensor_count * slot_cap, width_part), doc_rows.dtype)
        .at[flat_index]
        .set(doc_rows)
    )
    send_slots = (
        jnp.full((tensor_count * slot_cap,), row_count, jnp.int32).at[flat_index].set(block_slot)
    )
    got_rows, got_slots = (
        lax.all_to_all(
            send_rows.reshape(tensor_count, slot_cap, width_part),
            "tensor",
            split_axis=0,
            concat_axis=0,
            tiled=True,
        ),
        lax.all_to_all(
            send_slots.reshape(tensor_count, slot_cap),
            "tensor",
            split_axis=0,
            concat_axis=0,
            tiled=True,
        ),
    )
    packed_block = (
        jnp.zeros((row_count, width_part), doc_rows.dtype)
        .at[got_slots.reshape(-1)]
        .set(got_rows.reshape(-1, width_part), mode="drop")
    )
    shard_piece = lax.all_gather(packed_block, "tensor", axis=0, tiled=True)
    gate_part = jnp.dot(shard_piece, gate_weight, preferred_element_type=jnp.float32)
    up_part = jnp.dot(shard_piece, up_weight, preferred_element_type=jnp.float32)
    partial_sums = jnp.concatenate([gate_part, up_part], axis=1)
    share_sums = lax.psum_scatter(
        partial_sums.astype(jnp.bfloat16), "dp", scatter_dimension=0, tiled=True
    ).astype(jnp.float32)
    hidden_share = (jax.nn.silu(share_sums[:, :hidden_part]) * share_sums[:, hidden_part:]).astype(
        jnp.bfloat16
    )
    down_terms = jnp.dot(
        lax.all_gather(hidden_share, "dp", axis=0, tiled=True),
        down_weight,
        preferred_element_type=jnp.float32,
    )
    branch_out = lax.psum_scatter(
        down_terms.astype(jnp.bfloat16), "tensor", scatter_dimension=0, tiled=True
    ).astype(jnp.float32)
    return (packed_block.astype(jnp.float32) + branch_out).astype(jnp.bfloat16)


def solution(mesh):
    return jax.shard_map(
        local,
        mesh=mesh,
        in_specs=(
            P("tensor", "dp"),
            P("tensor"),
            P("dp", "tensor"),
            P("dp", "tensor"),
            P("tensor", "dp"),
        ),
        out_specs=P("tensor", "dp"),
        check_vma=False,
    )
```

profile of v0, /device:TPU:1, one launch (start us, length us, event | category | flops | bytes accessed | tf_op | source)
XLA Modules:
  0.0 336.3 jit_solution(10477875133898408064)
XLA Ops:
  6.5 0.7 and_select_fusion
  7.2 0.1 fusion.6
  7.3 0.1 reduce_window_sum.11
  7.4 0.2 select_reduce_fusion
  7.6 0.8 scatter_custom_fusion
  8.4 0.7 all_to_all.9
  9.0 6.8 %all-to-all-start = ((s32[16,1,8]{2,1,0:T(1,128)}), s32[16,1,8]{2,1,0:T(1,128)S(1)}, u32[]{:S(2)}, u32[]{:S(2)}) async-start(s32[16,1,8]{2,1,0:T(1,128)} %bitcast), calls=%async_computation | async-start | bytes 16384 | tf_op jit(solution)/shard_map/all_to_all | solution.py:37
  15.9 1.9 scatter_custom_fusion.1
  17.8 3.5 %all-to-all-done = s32[16,1,8]{2,1,0:T(1,128)S(1)} async-done(((s32[16,1,8]{2,1,0:T(1,128)}), s32[16,1,8]{2,1,0:T(1,128)S(1)}, u32[]{:S(2)}, u32[]{:S(2)}) %all-to-all-start) | async-done | bytes 544 | tf_op jit(solution)/shard_map/all_to_all | solution.py:37
  21.3 4.0 %all-to-all-start.1 = ((bf16[16,8,1024]{2,1,0:T(8,128)(2,1)}), bf16[16,8,1024]{2,1,0:T(8,128)(2,1)S(1)}, u32[]{:S(2)}, u32[]{:S(2)}) async-start(bf16[16,8,1024]{2,1,0:T(8,128)(2,1)} %bitcast.2), calls=%async_computation.1 | async-start | bytes 524288 | tf_op jit(solution)/shard_map/all_to_all | solution.py:30
  25.3 0.0 all-gather.3.cloned.1.call-start
  25.3 0.5 broadcast.66
  25.8 0.7 reduce.3
  26.5 0.1 reshape.43
  26.6 6.1 %all-to-all-done.1 = bf16[16,8,1024]{2,1,0:T(8,128)(2,1)S(1)} async-done(((bf16[16,8,1024]{2,1,0:T(8,128)(2,1)}), bf16[16,8,1024]{2,1,0:T(8,128)(2,1)S(1)}, u32[]{:S(2)}, u32[]{:S(2)}) %all-to-all-start.1) | async-done | bytes 262176 | tf_op jit(solution)/shard_map/all_to_all | solution.py:30
  32.7 1.7 scatter_custom_fusion.2
  34.5 0.0 reduce-scatter.3.cloned.1.call-start
  34.5 34.6 %all-gather.3.cloned.1.call-done = bf16[1024,1024]{1,0:T(8,128)(2,1)} async-done(((bf16[64,1024]{1,0:T(8,128)(2,1)}), bf16[1024,1024]{1,0:T(8,128)(2,1)}) %all-gather.3.cloned.1.call-update) | async-done | bytes 2097168 | tf_op jit(solution)/shard_map/all_gather | solution.py:50
  69.1 6.8 %convolution_convert_fusion = bf16[1024,1792]{1,0:T(8,128)(2,1)S(1)} fusion(bf16[1024,1024]{1,0:T(8,128)(2,1)} %all-gather.3.cloned.1.call-done, bf16[1024,1792]{1,0:T(8,128)(2,1)} %param.8), kind=kOutput, calls=%fused_computation.4 | convolution fusion | flops 3759931392 | bytes 9437184 | tf_op jit(solution)/shard_map/dot_general | solution.py:52
  75.9 5.4 %convolution_convert_fusion.1 = bf16[1024,1792]{1,0:T(8,128)(2,1)} fusion(bf16[1024,1024]{1,0:T(8,128)(2,1)S(1)} %copy-done.2, bf16[1024,1792]{1,0:T(8,128)(2,1)S(1)} %copy-done.1), kind=kOutput, calls=%fused_computation.5 | convolution fusion | flops 3759931392 | bytes 9437184 | tf_op jit(solution)/shard_map/dot_general | solution.py:51
  81.3 5.6 %pad_maximum_fusion = bf16[1024,3584]{1,0:T(8,128)(2,1)} fusion(bf16[1024,1792]{1,0:T(8,128)(2,1)S(1)} %convolution_convert_fusion, bf16[1024,1792]{1,0:T(8,128)(2,1)} %convolution_convert_fusion.1), kind=kLoop, calls=%fused_computation.3 | loop fusion | flops 14680064 | bytes 14680064 | tf_op jit(solution)/shard_map/concatenate | solution.py:53
  86.9 0.0 reduce-scatter.3.cloned.1.call-update
  86.9 0.0 all-gather.5.cloned.1.call-start
  87.0 106.5 %reduce-scatter.3.cloned.1.call-done = bf16[128,3584]{1,0:T(8,128)(2,1)} async-done(((bf16[1024,3584]{1,0:T(8,128)(2,1)}), bf16[128,3584]{1,0:T(8,128)(2,1)}) %reduce-scatter.3.cloned.1.call-update) | async-done | bytes 917520 | tf_op jit(solution)/shard_map/reduce_scatter | solution.py:54
  193.4 1.4 convert_element_type.24
  194.8 1.0 fusion
  195.9 0.0 reduce-scatter.5.cloned.1.call-start
  195.9 65.3 %all-gather.5.cloned.1.call-done = bf16[1024,1792]{1,0:T(8,128)(2,1)} async-done(((bf16[128,1792]{1,0:T(8,128)(2,1)}), bf16[1024,1792]{1,0:T(8,128)(2,1)}) %all-gather.5.cloned.1.call-update) | async-done | bytes 3670032 | tf_op jit(solution)/shard_map/all_gather | solution.py:61
  261.3 8.4 %convolution_convert_fusion.2 = bf16[1024,1024]{1,0:T(8,128)(2,1)} fusion(bf16[1024,1792]{1,0:T(8,128)(2,1)} %all-gather.5.cloned.1.call-done, bf16[1792,1024]{1,0:T(8,128)(2,1)} %param.9), kind=kOutput, calls=%fused_computation.6 | convolution fusion | flops 3759144960 | bytes 9437184 | tf_op jit(solution)/shard_map/dot_general | solution.py:60
  269.7 0.0 reduce-scatter.5.cloned.1.call-update
  269.7 58.5 %reduce-scatter.5.cloned.1.call-done = bf16[64,1024]{1,0:T(8,128)(2,1)} async-done(((bf16[1024,1024]{1,0:T(8,128)(2,1)}), bf16[64,1024]{1,0:T(8,128)(2,1)}) %reduce-scatter.5.cloned.1.call-update) | async-done | bytes 131088 | tf_op jit(solution)/shard_map/reduce_scatter | solution.py:65
  328.2 1.6 add_convert_fusion
  (10 shorter events, 0.1 us)
Async XLA Ops:
  9.0 12.2 %all-to-all-start = ((s32[16,1,8]{2,1,0:T(1,128)}), s32[16,1,8]{2,1,0:T(1,128)S(1)}, u32[]{:S(2)}, u32[]{:S(2)}) async-start(s32[16,1,8]{2,1,0:T(1,128)} %bitcast), calls=%async_computation | async-start | bytes 16384 | tf_op jit(solution)/shard_map/all_to_all | solution.py:37
  21.3 11.4 %all-to-all-start.1 = ((bf16[16,8,1024]{2,1,0:T(8,128)(2,1)}), bf16[16,8,1024]{2,1,0:T(8,128)(2,1)S(1)}, u32[]{:S(2)}, u32[]{:S(2)}) async-start(bf16[16,8,1024]{2,1,0:T(8,128)(2,1)} %bitcast.2), calls=%async_computation.1 | async-start | bytes 524288 | tf_op jit(solution)/shard_map/all_to_all | solution.py:30
  25.3 43.8 %all-gather.3.cloned.1.call-start = ((), (), s32[]{:S(2)}) async-start(), calls=%async_computation.4 | async-start | bytes 2228224 | tf_op jit(solution)/shard_map/all_gather | solution.py:50
  34.5 159.0 %reduce-scatter.3.cloned.1.call-start = ((), (), s32[]{:S(2)}) async-start(), calls=%async_computation.5 | async-start | bytes 8257536 | tf_op jit(solution)/shard_map/reduce_scatter | solution.py:54
  69.1 6.8 %copy-start.1 = (bf16[1024,1792]{1,0:T(8,128)(2,1)S(1)}, bf16[1024,1792]{1,0:T(8,128)(2,1)}, u32[]{:S(2)}) copy-start(bf16[1024,1792]{1,0:T(8,128)(2,1)} %param.7) | copy-start | bytes 11010052
  69.1 6.8 %copy-start.2 = (bf16[1024,1024]{1,0:T(8,128)(2,1)S(1)}, bf16[1024,1024]{1,0:T(8,128)(2,1)}, u32[]{:S(2)}) copy-start(bf16[1024,1024]{1,0:T(8,128)(2,1)} %all-gather.3.cloned.1.call-done) | copy-start | bytes 6291460
  86.9 174.4 %all-gather.5.cloned.1.call-start = ((), (), s32[]{:S(2)}) async-start(), calls=%async_computation.6 | async-start | bytes 4128768 | tf_op jit(solution)/shard_map/all_gather | solution.py:61
  195.9 132.3 %copy-start = (bf16[64,1024]{1,0:T(8,128)(2,1)S(1)}, bf16[64,1024]{1,0:T(8,128)(2,1)}, u32[]{:S(2)}) copy-start(bf16[64,1024]{1,0:T(8,128)(2,1)} %scatter_custom_fusion.2) | copy-start | bytes 393220
  195.9 132.3 %reduce-scatter.5.cloned.1.call-start = ((), (), s32[]{:S(2)}) async-start(), calls=%async_computation.7 | async-start | bytes 2228224 | tf_op jit(solution)/shard_map/reduce_scatter | solution.py:65
Sparse Core Ops, SparseCore 0:
  34.6 34.4 all-gather.2
  87.0 106.3 reduce-scatter.2
  196.0 65.2 all-gather.4
  269.9 58.2 reduce-scatter.4
where the time goes:
time: 340 us; the launch traced here: 336 us
  waiting for transfers between devices  275 us (81%)
  matrix products  20.6 us (6%)
  between operations  13.2 us (4%)
  other arithmetic  11.2 us (3%)
  starting transfers between devices  11 us (3%)
  local copies, waits for them, and re-layouts  5.72 us (2%)
    reduce_scatter x1, waiting for transfers between devices, local(): lax.psum_scatter(partial_sums.astype(jnp.bfloat16), 'dp', scatter_dimensi...  106 us
    all_gather x1, waiting for transfers between devices, local(): lax.all_gather(hidden_share, 'dp', axis=0, tiled=True)  65.3 us
    reduce_scatter x1, waiting for transfers between devices, local(): lax.psum_scatter(down_terms.astype(jnp.bfloat16), 'tensor', scatter_dimen...  58.5 us
    all_gather x1, waiting for transfers between devices, local(): shard_piece = lax.all_gather(packed_block, 'tensor', axis=0, tiled=True)  34.6 us
    dot_general x1, matrix products, local(): jnp.dot(lax.all_gather(hidden_share, 'dp', axis=0, tiled=True), down_weig...  8.45 us
    all_to_all x1, starting transfers between devices, local(): lax.all_to_all(send_slots.reshape(tensor_count, slot_cap), 'tensor', spli...  6.83 us
  transfers between devices with their start and end apart: 6, of which 6 were waited for; matrix products, arithmetic and copies ran while one was open for 1% of the time, Pallas kernels for 0%

commit v1 on v0

v1 whole, which is shorter than its diff:
```python
import functools

import jax
import jax.numpy as jnp
from jax import lax
from jax.experimental import pallas as pl
from jax.experimental.pallas import tpu as pltpu
from jax.sharding import PartitionSpec as P

MESH = pl.DeviceIdType.MESH
BF16 = jnp.bfloat16
F32 = jnp.float32

NC = 8
TILE = 256
TA = 4
TB = 3
CA = TA * TILE
CB = TB * TILE
HB2 = CB // 2
WIDTH = 1024
ROWS = 64

A_PT, A_PL, A_CB, A_Y = 0, 2, 4, 6
B_Y, B_PT, B_PL, B_CB = 7, 8, 10, 12
GA_Y, GA_Z, GA_F = 14, 15, 17
GB_Z, GB_F, GB_Y = 19, 21, 23
T_C, T_X, X_IN, X_CORE = 24, 25, 26, 27
KINDS = 28


def kernel(
    slot_ref, doc_ref, gate_ref, up_ref, down_ref, out_ref,
    w1, wd, xs_all, pa, pb,
    pt_a, pl_a, cs_a, cr_a, ys_a, yr_a,
    yr_b, q_b, pt_b, pl_b, cs_b, cr_b,
    ha, hb, o2, o2r, xs, xr, acc, ysnd, yrcv,
    snd, got, pos_s, pos_g,
    wsem, dsem, lsem, ssem, rsem, tsend, trecv, psend, precv, gsend, grecv,
):
    dp = lax.axis_index("dp")
    t = lax.axis_index("tensor")
    z, yh = dp // 2, dp % 2
    x, yl, core = t // 4, (t // 2) % 2, t % 2
    zn, zb, z2 = (z + 1) % 4, (z + 3) % 4, (z + 2) % 4
    dev_z = ((zn * 2 + yh, t), (zb * 2 + yh, t))
    dev_y = (z * 2 + 1 - yh, t)
    dev_core = (dp, t + 1 - 2 * core)
    dev_yl = (dp, t + 2 - 4 * yl)
    other = 1 - yh

    def dev_x(k):
        return (dp, ((x + k) % 4) * 4 + t % 4)

    def remote(src, dst, kind, c, device):
        return pltpu.make_async_remote_copy(
            src_ref=src, dst_ref=dst, send_sem=ssem.at[kind], recv_sem=rsem.at[kind, c],
            device_id=device, device_id_type=MESH,
        )

    def arrive(dst, kind, c):
        remote(dst, dst, kind, c, dev_y).wait_recv()

    own_x = xs_all.at[0, pl.ds(core * ROWS, ROWS)]
    doc_load = pltpu.make_async_copy(doc_ref, own_x, lsem)
    doc_load.start()

    def w_load(h, j):
        src = (gate_ref, up_ref)[h].at[:, pl.ds(pl.multiple_of(j * TILE, TILE), TILE)]
        return pltpu.make_async_copy(src, w1.at[h, j], wsem.at[h, j])

    def load_tile(j, carry):
        w_load(0, j).start()
        w_load(1, j).start()
        return carry

    lax.fori_loop(0, TA + TB, load_tile, 0)
    d_load = pltpu.make_async_copy(down_ref, wd, dsem)
    d_load.start()

    barrier = pltpu.get_barrier_semaphore()

    def greet(k, carry):
        pl.semaphore_signal(
            barrier, inc=1, device_id=(dp, (t + k) % 16), device_id_type=MESH
        )
        return carry

    lax.fori_loop(1, 16, greet, 0)
    for device in (dev_z[0], dev_z[1], dev_y):
        pl.semaphore_signal(barrier, inc=1, device_id=device, device_id_type=MESH)
    doc_load.wait()
    pl.semaphore_wait(barrier, 18)

    remote(own_x, own_x, X_CORE, 0, dev_core).start()
    remote(own_x, xs_all.at[1, pl.ds(core * ROWS, ROWS)], X_IN, 1, dev_yl).start()

    def x_slot(k, dy):
        return 2 * k + 1 - dy

    for k in (1, 3, 2):
        c = x_slot(k, 0)
        remote(own_x, xs_all.at[c, pl.ds(core * ROWS, ROWS)], X_IN, c, dev_x(4 - k)).start()

    def plan():
        slots = slot_ref[...]
        block = lax.shift_right_logical(slots, 6)
        place = slots & 63
        blocks = lax.broadcasted_iota(jnp.int32, (16, ROWS), 0)
        hot = jnp.where(blocks == block, 1.0, 0.0)
        before = jnp.where(
            lax.broadcasted_iota(jnp.int32, (ROWS, ROWS), 0)
            < lax.broadcasted_iota(jnp.int32, (ROWS, ROWS), 1),
            1.0,
            0.0,
        )
        count = jnp.dot(hot.astype(BF16), before.astype(BF16), preferred_element_type=F32)
        rank = jnp.sum(hot * count, axis=0, keepdims=True).astype(jnp.int32)
        return block, rank, place

    def placed(half):
        block, rank, _ = plan()
        q = lax.broadcasted_iota(jnp.int32, (256, ROWS), 0)
        return (block * 16 + half * 8 + rank) == q

    def send_places():
        _, _, place = plan()
        pick = placed(0) | placed(1)
        pos = jnp.sum(jnp.where(pick, place + 1, 0), axis=1, keepdims=True) - 1
        pos_s[...] = jnp.broadcast_to(pos, (256, 128))

        def one(k, carry):
            peer = (t + k) % 16
            place_copy(k, peer).start()
            return carry

        lax.fori_loop(1, 16, one, 0)
        pos_g[pl.ds(t * 16, 16)] = pos_s[pl.ds(t * 16, 16)]

    def place_copy(k, peer):
        return pltpu.make_async_remote_copy(
            src_ref=pos_s.at[pl.ds(peer * 16, 16)], dst_ref=pos_g.at[pl.ds(t * 16, 16)],
            send_sem=psend.at[k - 1], recv_sem=precv.at[k - 1], device_id=(dp, peer), device_id_type=MESH,
        )

    def place_arrive(k):
        rows = pos_g.at[pl.ds(((t + 16 - k) % 16) * 16, 16)]
        pltpu.make_async_remote_copy(
            src_ref=rows, dst_ref=rows, send_sem=psend.at[k - 1], recv_sem=precv.at[k - 1],
            device_id=dev_y, device_id_type=MESH,
        ).wait_recv()

    def row_copy(k, peer):
        return pltpu.make_async_remote_copy(
            src_ref=snd.at[pl.ds(peer * 16, 16)], dst_ref=got.at[pl.ds(t * 16, 16)],
            send_sem=gsend.at[k - 1], recv_sem=grecv.at[k - 1], device_id=(dp, peer), device_id_type=MESH,
        )

    def row_arrive(k):
        rows = got.at[pl.ds(((t + 16 - k) % 16) * 16, 16)]
        pltpu.make_async_remote_copy(
            src_ref=rows, dst_ref=rows, send_sem=gsend.at[k - 1], recv_sem=grecv.at[k - 1],
            device_id=dev_y, device_id_type=MESH,
        ).wait_recv()

    def stage0(c):
        arrive(xs_all.at[c, pl.ds((1 - core) * ROWS, ROWS)], X_CORE, c)

        def tile(j, dst, col):
            for h in range(2):
                @pl.when(c == 0)
                def _():
                    w_load(h, j).wait()

                r = jnp.dot(xs_all[c], w1[h, j], preferred_element_type=F32)
                dst[c, h, :, :, :, pl.ds(pl.multiple_of(col, TILE), TILE)] = r.astype(BF16).reshape(2, 4, 16, TILE)

        def tile_b(j, carry):
            tile(TA + j, pb, j * TILE)
            return carry

        def tile_a(j, carry):
            tile(j, pa, j * TILE)
            return carry

        lax.fori_loop(0, TA, tile_a, 0)
        for d in range(2):
            remote(pa.at[c, d, :, z2], pt_a.at[c, d], A_PT + d, c, dev_z[d]).start()
        for d in range(2):
            near = (zn, zb)[d]
            remote(pa.at[c, 1 - d, :, near], pl_a.at[c, d], A_PL + d, c, dev_z[d]).start()
        lax.fori_loop(0, TB, tile_b, 0)
        remote(pb.at[c, :, other], yr_b.at[c], B_Y, c, dev_y).start()

    def next_rows(c):
        rows = xs_all.at[c, pl.ds(core * ROWS, ROWS)]
        arrive(rows, X_IN, c)
        remote(rows, rows, X_CORE, c, dev_core).start()

        @pl.when(c == 1)
        def _():
            for k in (1, 3, 2):
                far = x_slot(k, 1)
                remote(rows, xs_all.at[far, pl.ds(core * ROWS, ROWS)], X_IN, far, dev_x(4 - k)).start()

    def stage1(c):
        for d in range(2):
            near = (zn, zb)[d]
            arrive(pt_a.at[c, d], A_PT + d, c)
            cs_a[c, d] = (pa[c, d, :, near].astype(F32) + pt_a[c, d].astype(F32)).astype(BF16)
            remote(cs_a.at[c, d], cr_a.at[c, d], A_CB + d, c, dev_z[d]).start()
        arrive(yr_b.at[c], B_Y, c)
        q_b[c] = (pb[c, :, yh].astype(F32) + yr_b[c].astype(F32)).astype(BF16)
        for d in range(2):
            remote(q_b.at[c, d, z2], pt_b.at[c, d], B_PT + d, c, dev_z[d]).start()
        for d in range(2):
            near = (zn, zb)[d]
            remote(q_b.at[c, 1 - d, near], pl_b.at[c, d], B_PL + d, c, dev_z[d]).start()

    def z_sum_a(c, h, y):
        return (
            pa[c, h, y, z].astype(F32)
            + cr_a[c, h, y].astype(F32)
            + pl_a[c, 1 - h, y].astype(F32)
        )

    def stage2(c):
        for d in range(2):
            near = (zn, zb)[d]
            arrive(pt_b.at[c, d], B_PT + d, c)
            cs_b[c, d] = (q_b[c, d, near].astype(F32) + pt_b[c, d].astype(F32)).astype(BF16)
            remote(cs_b.at[c, d], cr_b.at[c, d], B_CB + d, c, dev_z[d]).start()
        for d in range(2):
            arrive(pl_a.at[c, d], A_PL + d, c)
            arrive(cr_a.at[c, d], A_CB + d, c)
        for h in range(2):
            ys_a[c, h] = z_sum_a(c, h, other).astype(BF16)
        remote(ys_a.at[c], yr_a.at[c], A_Y, c, dev_y).start()

    def gated(g, u):
        return (g / (1.0 + jnp.exp(-g)) * u).astype(BF16)

    def stage3(c):
        for d in range(2):
            arrive(pl_b.at[c, d], B_PL + d, c)
            arrive(cr_b.at[c, d], B_CB + d, c)
        g, u = (
            q_b[c, h, z].astype(F32) + cr_b[c, h].astype(F32) + pl_b[c, 1 - h].astype(F32)
            for h in range(2)
        )
        hb[c, yh, z] = gated(g, u)
        for d in range(2):
            remote(hb.at[c, yh, z], hb.at[c, yh, z], GB_Z + d, c, dev_z[d]).start()
        arrive(yr_a.at[c], A_Y, c)
        g, u = (z_sum_a(c, h, yh) + yr_a[c, h].astype(F32) for h in range(2))
        ha[c, yh, z] = gated(g, u)
        remote(ha.at[c, yh, z], ha.at[c, yh, z], GA_Y, c, dev_y).start()

    def stage4(c):
        for d in range(2):
            back = (zb, zn)[d]
            arrive(hb.at[c, yh, back], GB_Z + d, c)
            part = hb.at[c, yh, back, :, pl.ds(d * HB2, HB2)]
            remote(part, part, GB_F + d, c, dev_z[d]).start()
        arrive(ha.at[c, other, z], GA_Y, c)
        for d in range(2):
            remote(ha.at[c, :, z], ha.at[c, :, z], GA_Z + d, c, dev_z[d]).start()

    def stage5(c):
        for d in range(2):
            arrive(hb.at[c, yh, z2, :, pl.ds(d * HB2, HB2)], GB_F + d, c)
        remote(hb.at[c, yh], hb.at[c, yh], GB_Y, c, dev_y).start()
        for d in range(2):
            back = (zb, zn)[d]
            arrive(ha.at[c, :, back], GA_Z + d, c)
            part = ha.at[c, d, back]
            remote(part, part, GA_F + d, c, dev_z[d]).start()

    def stage6(c):
        for d in range(2):
            arrive(ha.at[c, d, z2], GA_F + d, c)
        arrive(hb.at[c, other], GB_Y, c)

        @pl.when(c == 0)
        def _():
            d_load.wait()

        def tile(n, carry):
            cols = pl.ds(pl.multiple_of(n * TILE, TILE), TILE)
            r = jnp.dot(ha[c].reshape(128, CA), wd[0:CA, cols], preferred_element_type=F32)
            r += jnp.dot(hb[c].reshape(128, CB), wd[CA : CA + CB, cols], preferred_element_type=F32)
            o2[c, :, :, cols] = r.astype(BF16).reshape(2, ROWS, TILE)
            return carry

        lax.fori_loop(0, WIDTH // TILE, tile, 0)
        remote(o2.at[c, 1 - core], o2r.at[c], T_C, c, dev_core).start()

    def stage7(c):
        arrive(o2r.at[c], T_C, c)

        @pl.when(c < 2)
        def _():
            acc[c] = o2[c, core].astype(F32) + o2r[c].astype(F32)

        @pl.when(c >= 2)
        def _():
            xs[c] = (o2[c, core].astype(F32) + o2r[c].astype(F32)).astype(BF16)
            remote(xs.at[c], xr.at[c], T_X, c, dev_x(c // 2)).start()

    def yl_copy():
        return pltpu.make_async_remote_copy(
            src_ref=ysnd, dst_ref=yrcv, send_sem=tsend, recv_sem=trecv, device_id=dev_yl, device_id_type=MESH
        )

    def stage8(c):
        dy = (c + 1) % 2
        arrive(xr.at[c], T_X, c)
        acc[dy] = acc[dy] + xr[c].astype(F32)

        @pl.when(c == NC - 2)
        def _():
            ysnd[...] = acc[1].astype(BF16)
            yl_copy().start()

    stages = (stage0, stage1, stage2, stage3, stage4, stage5, stage6, stage7, stage8)

    def step(s, carry):
        for j, stage in enumerate(stages):
            c = s - j
            low = 2 if stage is stage8 else 0
            pl.when((c >= low) & (c < NC))(functools.partial(stage, c))
            if j == 0:

                @pl.when(s == 0)
                def _():
                    send_places()

                @pl.when(s < NC - 1)
                def _():
                    next_rows(s + 1)

        return carry

    lax.fori_loop(0, NC + len(stages) - 1, step, 0)

    yl_copy().wait_recv()
    rows = (
        xs_all[0, pl.ds(core * ROWS, ROWS)].astype(F32)
        + acc[0]
        + yrcv[...].astype(F32)
    ).astype(BF16)
    half = WIDTH // 2
    packed = jnp.dot(
        jnp.where(placed(0), 1.0, 0.0).astype(BF16), rows[:, :half], preferred_element_type=F32
    ) + jnp.dot(
        jnp.where(placed(1), 1.0, 0.0).astype(BF16), rows[:, half:], preferred_element_type=F32
    )
    snd[...] = packed.astype(BF16)

    def start_rows(k, carry):
        row_copy(k, (t + k) % 16).start()
        return carry

    lax.fori_loop(1, 16, start_rows, 0)
    got[pl.ds(t * 16, 16)] = snd[pl.ds(t * 16, 16)]

    def wait_places(k, carry):
        place_arrive(k)
        return carry

    lax.fori_loop(1, 16, wait_places, 0)
    slot_of = pos_g[:, 0:ROWS]
    q = lax.broadcasted_iota(jnp.int32, (256, ROWS), 0)
    here = slot_of == lax.broadcasted_iota(jnp.int32, (256, ROWS), 1)

    def wait_rows(k, carry):
        row_arrive(k)
        return carry

    lax.fori_loop(1, 16, wait_rows, 0)
    for part in range(2):
        pick = jnp.where(here & ((q // 8) % 2 == part), 1.0, 0.0).astype(BF16)
        out = lax.dot_general(
            pick, got[...], (((0,), (0,)), ((), ())), preferred_element_type=F32
        )
        out_ref[:, part * half : (part + 1) * half] = out.astype(BF16)

    def sent(ref, sem):
        pltpu.make_async_copy(ref, ref, sem).wait()

    for d in range(2):
        sent(pt_a.at[:, d], ssem.at[A_PT + d])
        sent(pl_a.at[:, d], ssem.at[A_PL + d])
        sent(cr_a.at[:, d], ssem.at[A_CB + d])
        sent(pt_b.at[:, d], ssem.at[B_PT + d])
        sent(pl_b.at[:, d], ssem.at[B_PL + d])
        sent(cr_b.at[:, d], ssem.at[B_CB + d])
        sent(ha.at[:, :, 0], ssem.at[GA_Z + d])
        sent(ha.at[:, 0, 0], ssem.at[GA_F + d])
        sent(hb.at[:, 0, 0], ssem.at[GB_Z + d])
        sent(hb.at[:, 0, 0, :, pl.ds(0, HB2)], ssem.at[GB_F + d])
    sent(yr_a, ssem.at[A_Y])
    sent(yr_b, ssem.at[B_Y])
    sent(ha.at[:, 0, 0], ssem.at[GA_Y])
    sent(hb.at[:, 0], ssem.at[GB_Y])
    sent(o2r, ssem.at[T_C])
    sent(xr.at[pl.ds(2, NC - 2)], ssem.at[T_X])
    sent(xs_all.at[:, pl.ds(0, ROWS)], ssem.at[X_CORE])
    sent(xs_all.at[pl.ds(1, NC - 1), pl.ds(0, ROWS)], ssem.at[X_IN])
    yl_copy().wait_send()

    def wait_sent(k, carry):
        peer = (t + k) % 16
        place_copy(k, peer).wait_send()
        row_copy(k, peer).wait_send()
        return carry

    lax.fori_loop(1, 16, wait_sent, 0)


def local(doc_rows, packed_slot, gate_weight, up_weight, down_weight):
    anywhere = pl.BlockSpec(memory_space=pl.ANY)
    vmem = pl.BlockSpec(memory_space=pltpu.VMEM)

    def buf(*shape, dtype=BF16):
        return pltpu.VMEM(shape, dtype)

    dma = pltpu.SemaphoreType.DMA
    return pl.pallas_call(
        kernel,
        out_shape=jax.ShapeDtypeStruct((ROWS, WIDTH), BF16),
        in_specs=[vmem, anywhere, anywhere, anywhere, anywhere],
        out_specs=vmem,
        scratch_shapes=[
            buf(2, TA + TB, WIDTH, TILE),
            buf(CA + CB, WIDTH),
            buf(NC, 128, WIDTH),
            buf(NC, 2, 2, 4, 16, CA),
            buf(NC, 2, 2, 4, 16, CB),
            buf(NC, 2, 2, 16, CA),
            buf(NC, 2, 2, 16, CA),
            buf(NC, 2, 2, 16, CA),
            buf(NC, 2, 2, 16, CA),
            buf(NC, 2, 16, CA),
            buf(NC, 2, 16, CA),
            buf(NC, 2, 4, 16, CB),
            buf(NC, 2, 4, 16, CB),
            buf(NC, 2, 16, CB),
            buf(NC, 2, 16, CB),
            buf(NC, 2, 16, CB),
            buf(NC, 2, 16, CB),
            buf(NC, 2, 4, 16, CA),
            buf(NC, 2, 4, 16, CB),
            buf(NC, 2, ROWS, WIDTH),
            buf(NC, ROWS, WIDTH),
            buf(NC, ROWS, WIDTH),
            buf(NC, ROWS, WIDTH),
            buf(2, ROWS, WIDTH, dtype=F32),
            buf(ROWS, WIDTH),
            buf(ROWS, WIDTH),
            buf(256, WIDTH // 2),
            buf(256, WIDTH // 2),
            buf(256, 128, dtype=jnp.int32),
            buf(256, 128, dtype=jnp.int32),
            dma((2, TA + TB)),
            dma,
            dma,
            dma((KINDS,)),
            dma((KINDS, NC)),
            dma,
            dma,
            dma((15,)),
            dma((15,)),
            dma((15,)),
            dma((15,)),
        ],
        compiler_params=pltpu.CompilerParams(
            collective_id=0, has_side_effects=True, vmem_limit_bytes=60 << 20
        ),
        cost_estimate=pl.CostEstimate(
            flops=2 * 1024 * 1024 * 5376, bytes_accessed=12 << 20, transcendentals=1024 * 1792 // 8
        ),
        name="layer",
    )(packed_slot.reshape(1, ROWS), doc_rows, gate_weight, up_weight, down_weight)


def solution(mesh):
    return jax.shard_map(
        local,
        mesh=mesh,
        in_specs=(
            P("tensor", "dp"),
            P("tensor"),
            P("dp", "tensor"),
            P("dp", "tensor"),
            P("tensor", "dp"),
        ),
        out_specs=P("tensor", "dp"),
        check_vma=False,
    )
```

time: 340 us -> 121 us (0.36); the launches traced: 336 us -> 121 us
  waiting for transfers between devices: 275 us -> 0 us
  Pallas kernels: 0 us -> 120 us
  matrix products: 20.6 us -> 0 us
  between operations: 13.2 us -> 0.01 us
  other arithmetic: 11.2 us -> 0 us
  starting transfers between devices: 11 us -> 0 us
  local copies, waits for them, and re-layouts: 5.72 us -> 1.57 us
    reduce_scatter x2 -> x0, waiting for transfers between devices: 165 us -> none  [the longest x1 106 us: local(): lax.psum_scatter(partial_sums.astype(jnp.bfloat16), 'dp', scatter_dimensi...]
    pallas_call x0 -> x1, Pallas kernels: none -> 120 us  [local(): pl.pallas_call(kernel, out_shape=jax.ShapeDtypeStruct((ROWS, WIDTH), BF16...]
    all_gather x2 -> x0, waiting for transfers between devices: 99.9 us -> none  [the longest x1 65.3 us: local(): lax.all_gather(hidden_share, 'dp', axis=0, tiled=True)]
    dot_general x3 -> x0, matrix products: 20.6 us -> none  [the longest x1 8.45 us: local(): jnp.dot(lax.all_gather(hidden_share, 'dp', axis=0, tiled=True), down_weig...]
    all_to_all x2 -> x0, starting transfers between devices: 10.8 us -> none  [the longest x1 6.83 us: local(): lax.all_to_all(send_slots.reshape(tensor_count, slot_cap), 'tensor', spli...]
    all_to_all x2 -> x0, waiting for transfers between devices: 9.62 us -> none  [the longest x1 6.13 us: local(): lax.all_to_all(send_rows.reshape(tensor_count, slot_cap, width_part), 'te...]
    concatenate x1 -> x0, other arithmetic: 5.57 us -> none  [local(): partial_sums = jnp.concatenate([gate_part, up_part], axis=1)]
    scatter x3 -> x0, local copies, waits for them, and re-layouts: 4.42 us -> none  [the longest x1 1.92 us: local(): send_rows = jnp.zeros((tensor_count * slot_cap, width_part), doc_rows.dty...]
  transfers between devices with their start and end apart: 6 -> 0, of which waited for: 6 -> 0; matrix products, arithmetic and copies ran while one was open for 1% -> 0% of each run, Pallas kernels for 0% -> 0%
where the time goes in v1:
time: 121 us
  Pallas kernels  120 us (99%)
  local copies, waits for them, and re-layouts  1.57 us (1%)
    pallas_call x1, Pallas kernels, local(): pl.pallas_call(kernel, out_shape=jax.ShapeDtypeStruct((ROWS, WIDTH), BF16...  120 us

profile of v1, /device:TPU:1, one launch (start us, length us, event | category | flops | bytes accessed | tf_op | source)
XLA Modules:
  0.0 121.1 jit_solution(7371153292141604535)
XLA Ops:
  0.0 119.6 %layer.1 = bf16[64,1024]{1,0:T(8,128)(2,1)} custom-call(s32[1,64]{1,0:T(1,128)} %bitcast.1, bf16[64,1024]{1,0:T(8,128)(2,1)} %doc_ref.1, bf16[1024,1792]{1,0:T(8,128)(2,1)} %gate_ref.1, bf16[1024,1792]{1,0:T(8,128)(2,1)} %up_ref.1, bf16[1792,1024]{1,0:T(8,128)(2,1)} %down_ref.1), custom_call_target="tpu_custom_call" | custom-call | flops 11274289152 | bytes 12582912 | tf_op jit(solution)/shard_map/layer/pallas_call | solution.py:429
  119.6 1.6 %copy.7 = bf16[64,1024]{1,0:T(8,128)(2,1)} copy(bf16[64,1024]{1,0:T(8,128)(2,1)} %layer.1) | data formatting | bytes 262144

commit v2 on v1

--- a/solution.py
+++ b/solution.py
@@ -1,5 +1,3 @@
-import functools
-
 import jax
 import jax.numpy as jnp
 from jax import lax
@@ -29,13 +27,24 @@
 KINDS = 28
 
 
+ORDER = (
+    0, 8, 19, 24, 17, 3, 23, 11, 7, 15, 21, 5, 13, 20, 31, 27, 136, 48, 29, 35,
+    18, 39, 4, 12, 53, 22, 2, 43, 37, 10, 55, 6, 36, 59, 45, 28, 26, 69, 51, 14,
+    1, 47, 44, 75, 9, 61, 34, 85, 52, 25, 42, 67, 77, 91, 60, 30, 101, 50, 38, 32,
+    68, 58, 93, 76, 71, 83, 54, 40, 46, 33, 66, 74, 84, 49, 99, 109, 137, 92, 70, 62,
+    63, 64, 41, 117, 82, 65, 100, 107, 90, 79, 87, 78, 57, 98, 115, 86, 108, 95, 56, 94,
+    116, 103, 73, 81, 106, 102, 114, 72, 80, 111, 89, 97, 124, 119, 88, 110, 96, 118, 105, 125,
+    122, 123, 104, 127, 113, 112, 126, 128,
+)
+
+
 def kernel(
     slot_ref, doc_ref, gate_ref, up_ref, down_ref, out_ref,
     w1, wd, xs_all, pa, pb,
     pt_a, pl_a, cs_a, cr_a, ys_a, yr_a,
     yr_b, q_b, pt_b, pl_b, cs_b, cr_b,
     ha, hb, o2, o2r, xs, xr, acc, ysnd, yrcv,
-    snd, got, pos_s, pos_g,
+    snd, got, pos_s, pos_g, pick_s, pick_r,
     wsem, dsem, lsem, ssem, rsem, tsend, trecv, psend, precv, gsend, grecv,
 ):
     dp = lax.axis_index("dp")
@@ -118,24 +127,34 @@
         rank = jnp.sum(hot * count, axis=0, keepdims=True).astype(jnp.int32)
         return block, rank, place
 
-    def placed(half):
-        block, rank, _ = plan()
+    def send_places():
+        block, rank, place = plan()
         q = lax.broadcasted_iota(jnp.int32, (256, ROWS), 0)
-        return (block * 16 + half * 8 + rank) == q
-
-    def send_places():
-        _, _, place = plan()
-        pick = placed(0) | placed(1)
-        pos = jnp.sum(jnp.where(pick, place + 1, 0), axis=1, keepdims=True) - 1
-        pos_s[...] = jnp.broadcast_to(pos, (256, 128))
+        home = block * 16 + rank
+        pos = 0
+        for half in range(2):
+            pick = home + half * 8 == q
+            pick_s[half] = jnp.where(pick, 1.0, 0.0).astype(BF16)
+            pos += jnp.sum(jnp.where(pick, place + 1, 0), axis=1, keepdims=True)
+        pos_s[...] = jnp.broadcast_to(pos - 1, (256, 128))
 
         def one(k, carry):
-            peer = (t + k) % 16
-            place_copy(k, peer).start()
+            place_copy(k, (t + k) % 16).start()
             return carry
 
         lax.fori_loop(1, 16, one, 0)
         pos_g[pl.ds(t * 16, 16)] = pos_s[pl.ds(t * 16, 16)]
+
+    def take_places():
+        def one(k, carry):
+            place_arrive(k)
+            return carry
+
+        lax.fori_loop(1, 16, one, 0)
+        q = lax.broadcasted_iota(jnp.int32, (256, ROWS), 0)
+        here = pos_g[:, 0:ROWS] == lax.broadcasted_iota(jnp.int32, (256, ROWS), 1)
+        for half in range(2):
+            pick_r[half] = jnp.where(here & ((q // 8) % 2 == half), 1.0, 0.0).astype(BF16)
 
     def place_copy(k, peer):
         return pltpu.make_async_remote_copy(
@@ -163,52 +182,57 @@
             device_id=dev_y, device_id_type=MESH,
         ).wait_recv()
 
-    def stage0(c):
+    first = set()
+
+    def once(name):
+        new = name not in first
+        first.add(name)
+        return new
+
+    def gate_up(c, dst, base, count):
+        fresh = once(base)
+
+        def tile(j, carry):
+            for h in range(2):
+                if fresh:
+                    w_load(h, base + j).wait()
+                r = jnp.dot(xs_all[c], w1[h, base + j], preferred_element_type=F32)
+                cols = pl.ds(pl.multiple_of(j * TILE, TILE), TILE)
+                dst[c, h, :, :, :, cols] = r.astype(BF16).reshape(2, 4, 16, TILE)
+            return carry
+
+        lax.fori_loop(0, count, tile, 0)
+
+    def step_0a(c):
         arrive(xs_all.at[c, pl.ds((1 - core) * ROWS, ROWS)], X_CORE, c)
-
-        def tile(j, dst, col):
-            for h in range(2):
-                @pl.when(c == 0)
-                def _():
-                    w_load(h, j).wait()
-
-                r = jnp.dot(xs_all[c], w1[h, j], preferred_element_type=F32)
-                dst[c, h, :, :, :, pl.ds(pl.multiple_of(col, TILE), TILE)] = r.astype(BF16).reshape(2, 4, 16, TILE)
-
-        def tile_b(j, carry):
-            tile(TA + j, pb, j * TILE)
-            return carry
-
-        def tile_a(j, carry):
-            tile(j, pa, j * TILE)
-            return carry
-
-        lax.fori_loop(0, TA, tile_a, 0)
+        gate_up(c, pa, 0, TA)
         for d in range(2):
             remote(pa.at[c, d, :, z2], pt_a.at[c, d], A_PT + d, c, dev_z[d]).start()
         for d in range(2):
             near = (zn, zb)[d]
             remote(pa.at[c, 1 - d, :, near], pl_a.at[c, d], A_PL + d, c, dev_z[d]).start()
-        lax.fori_loop(0, TB, tile_b, 0)
+
+    def step_0b(c):
+        gate_up(c, pb, TA, TB)
         remote(pb.at[c, :, other], yr_b.at[c], B_Y, c, dev_y).start()
 
     def next_rows(c):
         rows = xs_all.at[c, pl.ds(core * ROWS, ROWS)]
         arrive(rows, X_IN, c)
         remote(rows, rows, X_CORE, c, dev_core).start()
-
-        @pl.when(c == 1)
-        def _():
+        if c == 1:
             for k in (1, 3, 2):
                 far = x_slot(k, 1)
                 remote(rows, xs_all.at[far, pl.ds(core * ROWS, ROWS)], X_IN, far, dev_x(4 - k)).start()
 
-    def stage1(c):
+    def step_1a(c):
         for d in range(2):
             near = (zn, zb)[d]
             arrive(pt_a.at[c, d], A_PT + d, c)
             cs_a[c, d] = (pa[c, d, :, near].astype(F32) + pt_a[c, d].astype(F32)).astype(BF16)
             remote(cs_a.at[c, d], cr_a.at[c, d], A_CB + d, c, dev_z[d]).start()
+
+    def step_1b(c):
         arrive(yr_b.at[c], B_Y, c)
         q_b[c] = (pb[c, :, yh].astype(F32) + yr_b[c].astype(F32)).astype(BF16)
         for d in range(2):
@@ -224,12 +248,14 @@
             + pl_a[c, 1 - h, y].astype(F32)
         )
 
-    def stage2(c):
+    def step_2b(c):
         for d in range(2):
             near = (zn, zb)[d]
             arrive(pt_b.at[c, d], B_PT + d, c)
             cs_b[c, d] = (q_b[c, d, near].astype(F32) + pt_b[c, d].astype(F32)).astype(BF16)
             remote(cs_b.at[c, d], cr_b.at[c, d], B_CB + d, c, dev_z[d]).start()
+
+    def step_2a(c):
         for d in range(2):
             arrive(pl_a.at[c, d], A_PL + d, c)
             arrive(cr_a.at[c, d], A_CB + d, c)
@@ -240,7 +266,7 @@
     def gated(g, u):
         return (g / (1.0 + jnp.exp(-g)) * u).astype(BF16)
 
-    def stage3(c):
+    def step_3b(c):
         for d in range(2):
             arrive(pl_b.at[c, d], B_PL + d, c)
             arrive(cr_b.at[c, d], B_CB + d, c)
@@ -251,38 +277,42 @@
         hb[c, yh, z] = gated(g, u)
         for d in range(2):
             remote(hb.at[c, yh, z], hb.at[c, yh, z], GB_Z + d, c, dev_z[d]).start()
+
+    def step_3a(c):
         arrive(yr_a.at[c], A_Y, c)
         g, u = (z_sum_a(c, h, yh) + yr_a[c, h].astype(F32) for h in range(2))
         ha[c, yh, z] = gated(g, u)
         remote(ha.at[c, yh, z], ha.at[c, yh, z], GA_Y, c, dev_y).start()
 
-    def stage4(c):
+    def step_4b(c):
         for d in range(2):
             back = (zb, zn)[d]
             arrive(hb.at[c, yh, back], GB_Z + d, c)
             part = hb.at[c, yh, back, :, pl.ds(d * HB2, HB2)]
             remote(part, part, GB_F + d, c, dev_z[d]).start()
+
+    def step_4a(c):
         arrive(ha.at[c, other, z], GA_Y, c)
         for d in range(2):
             remote(ha.at[c, :, z], ha.at[c, :, z], GA_Z + d, c, dev_z[d]).start()
 
-    def stage5(c):
+    def step_5b(c):
         for d in range(2):
             arrive(hb.at[c, yh, z2, :, pl.ds(d * HB2, HB2)], GB_F + d, c)
         remote(hb.at[c, yh], hb.at[c, yh], GB_Y, c, dev_y).start()
+
+    def step_5a(c):
         for d in range(2):
             back = (zb, zn)[d]
             arrive(ha.at[c, :, back], GA_Z + d, c)
             part = ha.at[c, d, back]
             remote(part, part, GA_F + d, c, dev_z[d]).start()
 
-    def stage6(c):
+    def step_6(c):
         for d in range(2):
             arrive(ha.at[c, d, z2], GA_F + d, c)
         arrive(hb.at[c, other], GB_Y, c)
-
-        @pl.when(c == 0)
-        def _():
+        if once("down"):
             d_load.wait()
 
         def tile(n, carry):
@@ -295,53 +325,40 @@
         lax.fori_loop(0, WIDTH // TILE, tile, 0)
         remote(o2.at[c, 1 - core], o2r.at[c], T_C, c, dev_core).start()
 
-    def stage7(c):
+    def add(dy, value):
+        acc[dy] = value if once(("acc", dy)) else acc[dy] + value
+
+    def step_7(c):
         arrive(o2r.at[c], T_C, c)
-
-        @pl.when(c < 2)
-        def _():
-            acc[c] = o2[c, core].astype(F32) + o2r[c].astype(F32)
-
-        @pl.when(c >= 2)
-        def _():
-            xs[c] = (o2[c, core].astype(F32) + o2r[c].astype(F32)).astype(BF16)
+        total = o2[c, core].astype(F32) + o2r[c].astype(F32)
+        if c < 2:
+            add(c, total)
+        else:
+            xs[c] = total.astype(BF16)
             remote(xs.at[c], xr.at[c], T_X, c, dev_x(c // 2)).start()
+
+    def step_8(c):
+        arrive(xr.at[c], T_X, c)
+        add((c + 1) % 2, xr[c].astype(F32))
 
     def yl_copy():
         return pltpu.make_async_remote_copy(
             src_ref=ysnd, dst_ref=yrcv, send_sem=tsend, recv_sem=trecv, device_id=dev_yl, device_id_type=MESH
         )
 
-    def stage8(c):
-        dy = (c + 1) % 2
-        arrive(xr.at[c], T_X, c)
-        acc[dy] = acc[dy] + xr[c].astype(F32)
-
-        @pl.when(c == NC - 2)
-        def _():
-            ysnd[...] = acc[1].astype(BF16)
-            yl_copy().start()
-
-    stages = (stage0, stage1, stage2, stage3, stage4, stage5, stage6, stage7, stage8)
-
-    def step(s, carry):
-        for j, stage in enumerate(stages):
-            c = s - j
-            low = 2 if stage is stage8 else 0
-            pl.when((c >= low) & (c < NC))(functools.partial(stage, c))
-            if j == 0:
-
-                @pl.when(s == 0)
-                def _():
-                    send_places()
-
-                @pl.when(s < NC - 1)
-                def _():
-                    next_rows(s + 1)
-
-        return carry
-
-    lax.fori_loop(0, NC + len(stages) - 1, step, 0)
+    def step_y(c):
+        ysnd[...] = acc[1].astype(BF16)
+        yl_copy().start()
+
+    def step_p(c):
+        send_places() if c == 0 else take_places()
+
+    steps = (
+        step_0a, step_0b, next_rows, step_1a, step_1b, step_2b, step_2a, step_3b, step_3a,
+        step_4b, step_4a, step_5b, step_5a, step_6, step_7, step_8, step_y, step_p,
+    )
+    for entry in ORDER:
+        steps[entry // 8](entry % 8)
 
     yl_copy().wait_recv()
     rows = (
@@ -350,11 +367,8 @@
         + yrcv[...].astype(F32)
     ).astype(BF16)
     half = WIDTH // 2
-    packed = jnp.dot(
-        jnp.where(placed(0), 1.0, 0.0).astype(BF16), rows[:, :half], preferred_element_type=F32
-    ) + jnp.dot(
-        jnp.where(placed(1), 1.0, 0.0).astype(BF16), rows[:, half:], preferred_element_type=F32
-    )
+    packed = jnp.dot(pick_s[0], rows[:, :half], preferred_element_type=F32)
+    packed += jnp.dot(pick_s[1], rows[:, half:], preferred_element_type=F32)
     snd[...] = packed.astype(BF16)
 
     def start_rows(k, carry):
@@ -363,27 +377,6 @@
 
     lax.fori_loop(1, 16, start_rows, 0)
     got[pl.ds(t * 16, 16)] = snd[pl.ds(t * 16, 16)]
-
-    def wait_places(k, carry):
-        place_arrive(k)
-        return carry
-
-    lax.fori_loop(1, 16, wait_places, 0)
-    slot_of = pos_g[:, 0:ROWS]
-    q = lax.broadcasted_iota(jnp.int32, (256, ROWS), 0)
-    here = slot_of == lax.broadcasted_iota(jnp.int32, (256, ROWS), 1)
-
-    def wait_rows(k, carry):
-        row_arrive(k)
-        return carry
-
-    lax.fori_loop(1, 16, wait_rows, 0)
-    for part in range(2):
-        pick = jnp.where(here & ((q // 8) % 2 == part), 1.0, 0.0).astype(BF16)
-        out = lax.dot_general(
-            pick, got[...], (((0,), (0,)), ((), ())), preferred_element_type=F32
-        )
-        out_ref[:, part * half : (part + 1) * half] = out.astype(BF16)
 
     def sent(ref, sem):
         pltpu.make_async_copy(ref, ref, sem).wait()
@@ -412,10 +405,26 @@
     def wait_sent(k, carry):
         peer = (t + k) % 16
         place_copy(k, peer).wait_send()
-        row_copy(k, peer).wait_send()
         return carry
 
     lax.fori_loop(1, 16, wait_sent, 0)
+
+    def wait_rows(k, carry):
+        row_arrive(k)
+        return carry
+
+    lax.fori_loop(1, 16, wait_rows, 0)
+    for part in range(2):
+        out = lax.dot_general(
+            pick_r[part], got[...], (((0,), (0,)), ((), ())), preferred_element_type=F32
+        )
+        out_ref[:, part * half : (part + 1) * half] = out.astype(BF16)
+
+    def wait_rows_sent(k, carry):
+        row_copy(k, (t + k) % 16).wait_send()
+        return carry
+
+    lax.fori_loop(1, 16, wait_rows_sent, 0)
 
 
 def local(doc_rows, packed_slot, gate_weight, up_weight, down_weight):
@@ -462,6 +471,8 @@
             buf(256, WIDTH // 2),
             buf(256, 128, dtype=jnp.int32),
             buf(256, 128, dtype=jnp.int32),
+            buf(2, 256, ROWS),
+            buf(2, 256, ROWS),
             dma((2, TA + TB)),
             dma,
             dma,

time: 121 us -> 109 us (0.901)
  Pallas kernels: 120 us -> 107 us
    pallas_call x1, Pallas kernels: 120 us -> 107 us  [local(): pl.pallas_call(kernel, out_shape=jax.ShapeDtypeStruct((ROWS, WIDTH), BF16...]
where the time goes in v2:
time: 109 us
  Pallas kernels  107 us (98%)
  local copies, waits for them, and re-layouts  1.57 us (1%)
    pallas_call x1, Pallas kernels, local(): pl.pallas_call(kernel, out_shape=jax.ShapeDtypeStruct((ROWS, WIDTH), BF16...  107 us

profile of v2, /device:TPU:1, one launch (start us, length us, event | category | flops | bytes accessed | tf_op | source)
XLA Modules:
  0.0 108.8 jit_solution(9003721890492081242)
XLA Ops:
  0.0 107.2 %layer.1 = bf16[64,1024]{1,0:T(8,128)(2,1)} custom-call(s32[1,64]{1,0:T(1,128)} %bitcast.1, bf16[64,1024]{1,0:T(8,128)(2,1)} %doc_ref.1, bf16[1024,1792]{1,0:T(8,128)(2,1)} %gate_ref.1, bf16[1024,1792]{1,0:T(8,128)(2,1)} %up_ref.1, bf16[1792,1024]{1,0:T(8,128)(2,1)} %down_ref.1), custom_call_target="tpu_custom_call" | custom-call | flops 11274289152 | bytes 12582912 | tf_op jit(solution)/shard_map/layer/pallas_call | solution.py:438
  107.2 1.6 %copy.7 = bf16[64,1024]{1,0:T(8,128)(2,1)} copy(bf16[64,1024]{1,0:T(8,128)(2,1)} %layer.1) | data formatting | bytes 262144

commit v3 on v2

--- a/solution.py
+++ b/solution.py
@@ -28,14 +28,16 @@
 
 
 ORDER = (
-    0, 8, 19, 24, 17, 3, 23, 11, 7, 15, 21, 5, 13, 20, 31, 27, 136, 48, 29, 35,
-    18, 39, 4, 12, 53, 22, 2, 43, 37, 10, 55, 6, 36, 59, 45, 28, 26, 69, 51, 14,
-    1, 47, 44, 75, 9, 61, 34, 85, 52, 25, 42, 67, 77, 91, 60, 30, 101, 50, 38, 32,
-    68, 58, 93, 76, 71, 83, 54, 40, 46, 33, 66, 74, 84, 49, 99, 109, 137, 92, 70, 62,
-    63, 64, 41, 117, 82, 65, 100, 107, 90, 79, 87, 78, 57, 98, 115, 86, 108, 95, 56, 94,
-    116, 103, 73, 81, 106, 102, 114, 72, 80, 111, 89, 97, 124, 119, 88, 110, 96, 118, 105, 125,
-    122, 123, 104, 127, 113, 112, 126, 128,
+    0, 8, 17, 19, 1, 23, 9, 3, 18, 11, 22, 7, 27, 2, 136, 10, 21, 33, 31, 6,
+    24, 35, 15, 51, 20, 26, 14, 4, 5, 12, 13, 34, 43, 28, 39, 38, 42, 67, 36, 30,
+    59, 55, 50, 52, 46, 25, 58, 44, 47, 37, 75, 48, 29, 41, 66, 49, 83, 54, 68, 45,
+    74, 60, 82, 62, 63, 91, 57, 99, 70, 71, 84, 61, 53, 64, 90, 76, 137, 98, 78, 32,
+    86, 65, 107, 69, 79, 92, 100, 115, 77, 87, 106, 40, 73, 94, 102, 85, 95, 81, 93, 114,
+    108, 103, 56, 116, 110, 89, 101, 118, 97, 80, 111, 72, 123, 122, 88, 119, 109, 105, 124, 117,
+    126, 113, 128, 96, 104, 127, 112, 125,
 )
+DIRECT_SUM = (0,)
+DIRECT_GATHER = (0,)
 
 
 def kernel(
@@ -53,6 +55,7 @@
     x, yl, core = t // 4, (t // 2) % 2, t % 2
     zn, zb, z2 = (z + 1) % 4, (z + 3) % 4, (z + 2) % 4
     dev_z = ((zn * 2 + yh, t), (zb * 2 + yh, t))
+    dev_z2 = (z2 * 2 + yh, t)
     dev_y = (z * 2 + 1 - yh, t)
     dev_core = (dp, t + 1 - 2 * core)
     dev_yl = (dp, t + 2 - 4 * yl)
@@ -96,10 +99,10 @@
         return carry
 
     lax.fori_loop(1, 16, greet, 0)
-    for device in (dev_z[0], dev_z[1], dev_y):
+    for device in (dev_z[0], dev_z[1], dev_z2, dev_y):
         pl.semaphore_signal(barrier, inc=1, device_id=device, device_id_type=MESH)
     doc_load.wait()
-    pl.semaphore_wait(barrier, 18)
+    pl.semaphore_wait(barrier, 19)
 
     remote(own_x, own_x, X_CORE, 0, dev_core).start()
     remote(own_x, xs_all.at[1, pl.ds(core * ROWS, ROWS)], X_IN, 1, dev_yl).start()
@@ -207,10 +210,13 @@
         arrive(xs_all.at[c, pl.ds((1 - core) * ROWS, ROWS)], X_CORE, c)
         gate_up(c, pa, 0, TA)
         for d in range(2):
-            remote(pa.at[c, d, :, z2], pt_a.at[c, d], A_PT + d, c, dev_z[d]).start()
+            via = dev_z2 if c in DIRECT_SUM else dev_z[d]
+            remote(pa.at[c, d, :, z2], pt_a.at[c, d], A_PT + d, c, via).start()
         for d in range(2):
             near = (zn, zb)[d]
             remote(pa.at[c, 1 - d, :, near], pl_a.at[c, d], A_PL + d, c, dev_z[d]).start()
+            if c in DIRECT_SUM:
+                remote(pa.at[c, d, :, near], cr_a.at[c, d], A_CB + d, c, dev_z[d]).start()
 
     def step_0b(c):
         gate_up(c, pb, TA, TB)
@@ -229,6 +235,8 @@
         for d in range(2):
             near = (zn, zb)[d]
             arrive(pt_a.at[c, d], A_PT + d, c)
+            if c in DIRECT_SUM:
+                continue
             cs_a[c, d] = (pa[c, d, :, near].astype(F32) + pt_a[c, d].astype(F32)).astype(BF16)
             remote(cs_a.at[c, d], cr_a.at[c, d], A_CB + d, c, dev_z[d]).start()
 
@@ -242,11 +250,12 @@
             remote(q_b.at[c, 1 - d, near], pl_b.at[c, d], B_PL + d, c, dev_z[d]).start()
 
     def z_sum_a(c, h, y):
-        return (
+        total = (
             pa[c, h, y, z].astype(F32)
             + cr_a[c, h, y].astype(F32)
             + pl_a[c, 1 - h, y].astype(F32)
         )
+        return total + pt_a[c, h, y].astype(F32) if c in DIRECT_SUM else total
 
     def step_2b(c):
         for d in range(2):
@@ -277,6 +286,10 @@
         hb[c, yh, z] = gated(g, u)
         for d in range(2):
             remote(hb.at[c, yh, z], hb.at[c, yh, z], GB_Z + d, c, dev_z[d]).start()
+        if c in DIRECT_GATHER:
+            for d in range(2):
+                part = hb.at[c, yh, z, :, pl.ds(d * HB2, HB2)]
+                remote(part, part, GB_F + d, c, dev_z2).start()
 
     def step_3a(c):
         arrive(yr_a.at[c], A_Y, c)
@@ -288,6 +301,8 @@
         for d in range(2):
             back = (zb, zn)[d]
             arrive(hb.at[c, yh, back], GB_Z + d, c)
+            if c in DIRECT_GATHER:
+                continue
             part = hb.at[c, yh, back, :, pl.ds(d * HB2, HB2)]
             remote(part, part, GB_F + d, c, dev_z[d]).start()
 
@@ -295,6 +310,9 @@
         arrive(ha.at[c, other, z], GA_Y, c)
         for d in range(2):
             remote(ha.at[c, :, z], ha.at[c, :, z], GA_Z + d, c, dev_z[d]).start()
+        if c in DIRECT_GATHER:
+            for d in range(2):
+                remote(ha.at[c, d, z], ha.at[c, d, z], GA_F + d, c, dev_z2).start()
 
     def step_5b(c):
         for d in range(2):
@@ -305,6 +323,8 @@
         for d in range(2):
             back = (zb, zn)[d]
             arrive(ha.at[c, :, back], GA_Z + d, c)
+            if c in DIRECT_GATHER:
+                continue
             part = ha.at[c, d, back]
             remote(part, part, GA_F + d, c, dev_z[d]).start()
 
@@ -371,7 +391,8 @@
     packed += jnp.dot(pick_s[1], rows[:, half:], preferred_element_type=F32)
     snd[...] = packed.astype(BF16)
 
-    def start_rows(k, carry):
+    def start_rows(i, carry):
+        k = (i + 6) % 15 + 1
         row_copy(k, (t + k) % 16).start()
         return carry
 

time: 109 us -> 104 us (0.954)
  Pallas kernels: 107 us -> 103 us
    pallas_call x1, Pallas kernels: 107 us -> 103 us  [local(): pl.pallas_call(kernel, out_shape=jax.ShapeDtypeStruct((ROWS, WIDTH), BF16...]
where the time goes in v3:
time: 104 us
  Pallas kernels  103 us (99%)
  local copies, waits for them, and re-layouts  1.57 us (2%)
    pallas_call x1, Pallas kernels, local(): pl.pallas_call(kernel, out_shape=jax.ShapeDtypeStruct((ROWS, WIDTH), BF16...  103 us

profile of v3, /device:TPU:1, one launch (start us, length us, event | category | flops | bytes accessed | tf_op | source)
XLA Modules:
  0.0 104.1 jit_solution(2226917443152900796)
XLA Ops:
  0.0 102.5 %layer.1 = bf16[64,1024]{1,0:T(8,128)(2,1)} custom-call(s32[1,64]{1,0:T(1,128)} %bitcast.1, bf16[64,1024]{1,0:T(8,128)(2,1)} %doc_ref.1, bf16[1024,1792]{1,0:T(8,128)(2,1)} %gate_ref.1, bf16[1024,1792]{1,0:T(8,128)(2,1)} %up_ref.1, bf16[1792,1024]{1,0:T(8,128)(2,1)} %down_ref.1), custom_call_target="tpu_custom_call" | custom-call | flops 11274289152 | bytes 12582912 | tf_op jit(solution)/shard_map/layer/pallas_call | solution.py:459
  102.6 1.6 %copy.7 = bf16[64,1024]{1,0:T(8,128)(2,1)} copy(bf16[64,1024]{1,0:T(8,128)(2,1)} %layer.1) | data formatting | bytes 262144

commit v4 on v3

--- a/solution.py
+++ b/solution.py
@@ -19,22 +19,22 @@
 WIDTH = 1024
 ROWS = 64
 
-A_PT, A_PL, A_CB, A_Y = 0, 2, 4, 6
-B_Y, B_PT, B_PL, B_CB = 7, 8, 10, 12
-GA_Y, GA_Z, GA_F = 14, 15, 17
-GB_Z, GB_F, GB_Y = 19, 21, 23
-T_C, T_X, X_IN, X_CORE = 24, 25, 26, 27
-KINDS = 28
+A_PT, A_PL, A_CB, A_Y, B_Y, B_PT, B_PL, B_CB = (0, 0), (1, 1), (2, 1), (3, 2), (4, 3), (5, 4), (6, 5), (7, 5)
+GA_Y, GA_F, GB_F, GB_Y = (8, 6), (9, 7), (10, 8), (11, 9)
+T_C, T_X, X_IN, X_CORE = (12, 10), (13, 11), (14, 12), (15, 13)
+GA_Z = ((16, 14), (16, 15))
+GB_Z = ((17, 16), (17, 17))
+KINDS = 18
 
 
 ORDER = (
-    0, 8, 17, 19, 1, 23, 9, 3, 18, 11, 22, 7, 27, 2, 136, 10, 21, 33, 31, 6,
-    24, 35, 15, 51, 20, 26, 14, 4, 5, 12, 13, 34, 43, 28, 39, 38, 42, 67, 36, 30,
-    59, 55, 50, 52, 46, 25, 58, 44, 47, 37, 75, 48, 29, 41, 66, 49, 83, 54, 68, 45,
-    74, 60, 82, 62, 63, 91, 57, 99, 70, 71, 84, 61, 53, 64, 90, 76, 137, 98, 78, 32,
-    86, 65, 107, 69, 79, 92, 100, 115, 77, 87, 106, 40, 73, 94, 102, 85, 95, 81, 93, 114,
-    108, 103, 56, 116, 110, 89, 101, 118, 97, 80, 111, 72, 123, 122, 88, 119, 109, 105, 124, 117,
-    126, 113, 128, 96, 104, 127, 112, 125,
+    0, 8, 136, 17, 19, 1, 3, 11, 24, 23, 7, 15, 18, 27, 20, 4, 12, 2, 48, 51,
+    35, 10, 31, 22, 36, 28, 21, 6, 5, 14, 137, 13, 43, 44, 52, 67, 34, 26, 38, 9,
+    60, 59, 42, 39, 29, 30, 46, 50, 68, 55, 47, 25, 58, 32, 53, 62, 76, 54, 37, 84,
+    66, 75, 33, 83, 71, 74, 92, 70, 63, 45, 100, 78, 49, 82, 91, 41, 69, 79, 99, 90,
+    61, 86, 108, 98, 57, 65, 87, 40, 94, 95, 107, 77, 116, 102, 85, 106, 103, 115, 64, 93,
+    73, 81, 56, 114, 110, 101, 89, 111, 97, 118, 124, 80, 109, 72, 119, 88, 105, 122, 96, 117,
+    126, 113, 128, 104, 112, 123, 125, 127,
 )
 DIRECT_SUM = (0,)
 DIRECT_GATHER = (0,)
@@ -43,8 +43,8 @@
 def kernel(
     slot_ref, doc_ref, gate_ref, up_ref, down_ref, out_ref,
     w1, wd, xs_all, pa, pb,
-    pt_a, pl_a, cs_a, cr_a, ys_a, yr_a,
-    yr_b, q_b, pt_b, pl_b, cs_b, cr_b,
+    pt_a, pc_a, cs_a, ys_a, yr_a,
+    yr_b, q_b, pt_b, pc_b, cs_b,
     ha, hb, o2, o2r, xs, xr, acc, ysnd, yrcv,
     snd, got, pos_s, pos_g, pick_s, pick_r,
     wsem, dsem, lsem, ssem, rsem, tsend, trecv, psend, precv, gsend, grecv,
@@ -66,7 +66,7 @@
 
     def remote(src, dst, kind, c, device):
         return pltpu.make_async_remote_copy(
-            src_ref=src, dst_ref=dst, send_sem=ssem.at[kind], recv_sem=rsem.at[kind, c],
+            src_ref=src, dst_ref=dst, send_sem=ssem.at[kind[0]], recv_sem=rsem.at[kind[1], c],
             device_id=device, device_id_type=MESH,
         )
 
@@ -79,7 +79,7 @@
 
     def w_load(h, j):
         src = (gate_ref, up_ref)[h].at[:, pl.ds(pl.multiple_of(j * TILE, TILE), TILE)]
-        return pltpu.make_async_copy(src, w1.at[h, j], wsem.at[h, j])
+        return pltpu.make_async_copy(src, w1.at[h, j], wsem.at[j])
 
     def load_tile(j, carry):
         w_load(0, j).start()
@@ -149,11 +149,7 @@
         pos_g[pl.ds(t * 16, 16)] = pos_s[pl.ds(t * 16, 16)]
 
     def take_places():
-        def one(k, carry):
-            place_arrive(k)
-            return carry
-
-        lax.fori_loop(1, 16, one, 0)
+        all_peers(pos_g, precv)
         q = lax.broadcasted_iota(jnp.int32, (256, ROWS), 0)
         here = pos_g[:, 0:ROWS] == lax.broadcasted_iota(jnp.int32, (256, ROWS), 1)
         for half in range(2):
@@ -162,28 +158,18 @@
     def place_copy(k, peer):
         return pltpu.make_async_remote_copy(
             src_ref=pos_s.at[pl.ds(peer * 16, 16)], dst_ref=pos_g.at[pl.ds(t * 16, 16)],
-            send_sem=psend.at[k - 1], recv_sem=precv.at[k - 1], device_id=(dp, peer), device_id_type=MESH,
-        )
-
-    def place_arrive(k):
-        rows = pos_g.at[pl.ds(((t + 16 - k) % 16) * 16, 16)]
-        pltpu.make_async_remote_copy(
-            src_ref=rows, dst_ref=rows, send_sem=psend.at[k - 1], recv_sem=precv.at[k - 1],
-            device_id=dev_y, device_id_type=MESH,
-        ).wait_recv()
+            send_sem=psend, recv_sem=precv, device_id=(dp, peer), device_id_type=MESH,
+        )
 
     def row_copy(k, peer):
         return pltpu.make_async_remote_copy(
             src_ref=snd.at[pl.ds(peer * 16, 16)], dst_ref=got.at[pl.ds(t * 16, 16)],
-            send_sem=gsend.at[k - 1], recv_sem=grecv.at[k - 1], device_id=(dp, peer), device_id_type=MESH,
-        )
-
-    def row_arrive(k):
-        rows = got.at[pl.ds(((t + 16 - k) % 16) * 16, 16)]
-        pltpu.make_async_remote_copy(
-            src_ref=rows, dst_ref=rows, send_sem=gsend.at[k - 1], recv_sem=grecv.at[k - 1],
-            device_id=dev_y, device_id_type=MESH,
-        ).wait_recv()
+            send_sem=gsend, recv_sem=grecv, device_id=(dp, peer), device_id_type=MESH,
+        )
+
+    def all_peers(ref, sem):
+        rows = ref.at[pl.ds(0, 240)]
+        pltpu.make_async_copy(rows, rows, sem).wait()
 
     first = set()
 
@@ -196,9 +182,10 @@
         fresh = once(base)
 
         def tile(j, carry):
+            if fresh:
+                pair = w1.at[:, base + j]
+                pltpu.make_async_copy(pair, pair, wsem.at[base + j]).wait()
             for h in range(2):
-                if fresh:
-                    w_load(h, base + j).wait()
                 r = jnp.dot(xs_all[c], w1[h, base + j], preferred_element_type=F32)
                 cols = pl.ds(pl.multiple_of(j * TILE, TILE), TILE)
                 dst[c, h, :, :, :, cols] = r.astype(BF16).reshape(2, 4, 16, TILE)
@@ -211,12 +198,12 @@
         gate_up(c, pa, 0, TA)
         for d in range(2):
             via = dev_z2 if c in DIRECT_SUM else dev_z[d]
-            remote(pa.at[c, d, :, z2], pt_a.at[c, d], A_PT + d, c, via).start()
+            remote(pa.at[c, d, :, z2], pt_a.at[c, d], A_PT, c, via).start()
         for d in range(2):
             near = (zn, zb)[d]
-            remote(pa.at[c, 1 - d, :, near], pl_a.at[c, d], A_PL + d, c, dev_z[d]).start()
+            remote(pa.at[c, 1 - d, :, near], pc_a.at[c, 0, d], A_PL, c, dev_z[d]).start()
             if c in DIRECT_SUM:
-                remote(pa.at[c, d, :, near], cr_a.at[c, d], A_CB + d, c, dev_z[d]).start()
+                remote(pa.at[c, d, :, near], pc_a.at[c, 1, d], A_CB, c, dev_z[d]).start()
 
     def step_0b(c):
         gate_up(c, pb, TA, TB)
@@ -232,42 +219,40 @@
                 remote(rows, xs_all.at[far, pl.ds(core * ROWS, ROWS)], X_IN, far, dev_x(4 - k)).start()
 
     def step_1a(c):
+        arrive(pt_a.at[c], A_PT, c)
+        if c in DIRECT_SUM:
+            return
         for d in range(2):
             near = (zn, zb)[d]
-            arrive(pt_a.at[c, d], A_PT + d, c)
-            if c in DIRECT_SUM:
-                continue
             cs_a[c, d] = (pa[c, d, :, near].astype(F32) + pt_a[c, d].astype(F32)).astype(BF16)
-            remote(cs_a.at[c, d], cr_a.at[c, d], A_CB + d, c, dev_z[d]).start()
+            remote(cs_a.at[c, d], pc_a.at[c, 1, d], A_CB, c, dev_z[d]).start()
 
     def step_1b(c):
         arrive(yr_b.at[c], B_Y, c)
         q_b[c] = (pb[c, :, yh].astype(F32) + yr_b[c].astype(F32)).astype(BF16)
         for d in range(2):
-            remote(q_b.at[c, d, z2], pt_b.at[c, d], B_PT + d, c, dev_z[d]).start()
+            remote(q_b.at[c, d, z2], pt_b.at[c, d], B_PT, c, dev_z[d]).start()
         for d in range(2):
             near = (zn, zb)[d]
-            remote(q_b.at[c, 1 - d, near], pl_b.at[c, d], B_PL + d, c, dev_z[d]).start()
+            remote(q_b.at[c, 1 - d, near], pc_b.at[c, 0, d], B_PL, c, dev_z[d]).start()
 
     def z_sum_a(c, h, y):
         total = (
             pa[c, h, y, z].astype(F32)
-            + cr_a[c, h, y].astype(F32)
-            + pl_a[c, 1 - h, y].astype(F32)
+            + pc_a[c, 1, h, y].astype(F32)
+            + pc_a[c, 0, 1 - h, y].astype(F32)
         )
         return total + pt_a[c, h, y].astype(F32) if c in DIRECT_SUM else total
 
     def step_2b(c):
+        arrive(pt_b.at[c], B_PT, c)
         for d in range(2):
             near = (zn, zb)[d]
-            arrive(pt_b.at[c, d], B_PT + d, c)
             cs_b[c, d] = (q_b[c, d, near].astype(F32) + pt_b[c, d].astype(F32)).astype(BF16)
-            remote(cs_b.at[c, d], cr_b.at[c, d], B_CB + d, c, dev_z[d]).start()
+            remote(cs_b.at[c, d], pc_b.at[c, 1, d], B_CB, c, dev_z[d]).start()
 
     def step_2a(c):
-        for d in range(2):
-            arrive(pl_a.at[c, d], A_PL + d, c)
-            arrive(cr_a.at[c, d], A_CB + d, c)
+        arrive(pc_a.at[c], A_PL, c)
         for h in range(2):
             ys_a[c, h] = z_sum_a(c, h, other).astype(BF16)
         remote(ys_a.at[c], yr_a.at[c], A_Y, c, dev_y).start()
@@ -276,20 +261,18 @@
         return (g / (1.0 + jnp.exp(-g)) * u).astype(BF16)
 
     def step_3b(c):
-        for d in range(2):
-            arrive(pl_b.at[c, d], B_PL + d, c)
-            arrive(cr_b.at[c, d], B_CB + d, c)
+        arrive(pc_b.at[c], B_PL, c)
         g, u = (
-            q_b[c, h, z].astype(F32) + cr_b[c, h].astype(F32) + pl_b[c, 1 - h].astype(F32)
+            q_b[c, h, z].astype(F32) + pc_b[c, 1, h].astype(F32) + pc_b[c, 0, 1 - h].astype(F32)
             for h in range(2)
         )
         hb[c, yh, z] = gated(g, u)
         for d in range(2):
-            remote(hb.at[c, yh, z], hb.at[c, yh, z], GB_Z + d, c, dev_z[d]).start()
+            remote(hb.at[c, yh, z], hb.at[c, yh, z], GB_Z[d], c, dev_z[d]).start()
         if c in DIRECT_GATHER:
             for d in range(2):
                 part = hb.at[c, yh, z, :, pl.ds(d * HB2, HB2)]
-                remote(part, part, GB_F + d, c, dev_z2).start()
+                remote(part, part, GB_F, c, dev_z2).start()
 
     def step_3a(c):
         arrive(yr_a.at[c], A_Y, c)
@@ -300,37 +283,35 @@
     def step_4b(c):
         for d in range(2):
             back = (zb, zn)[d]
-            arrive(hb.at[c, yh, back], GB_Z + d, c)
+            arrive(hb.at[c, yh, back], GB_Z[d], c)
             if c in DIRECT_GATHER:
                 continue
             part = hb.at[c, yh, back, :, pl.ds(d * HB2, HB2)]
-            remote(part, part, GB_F + d, c, dev_z[d]).start()
+            remote(part, part, GB_F, c, dev_z[d]).start()
 
     def step_4a(c):
         arrive(ha.at[c, other, z], GA_Y, c)
         for d in range(2):
-            remote(ha.at[c, :, z], ha.at[c, :, z], GA_Z + d, c, dev_z[d]).start()
+            remote(ha.at[c, :, z], ha.at[c, :, z], GA_Z[d], c, dev_z[d]).start()
         if c in DIRECT_GATHER:
             for d in range(2):
-                remote(ha.at[c, d, z], ha.at[c, d, z], GA_F + d, c, dev_z2).start()
+                remote(ha.at[c, d, z], ha.at[c, d, z], GA_F, c, dev_z2).start()
 
     def step_5b(c):
-        for d in range(2):
-            arrive(hb.at[c, yh, z2, :, pl.ds(d * HB2, HB2)], GB_F + d, c)
+        arrive(hb.at[c, yh, z2], GB_F, c)
         remote(hb.at[c, yh], hb.at[c, yh], GB_Y, c, dev_y).start()
 
     def step_5a(c):
         for d in range(2):
             back = (zb, zn)[d]
-            arrive(ha.at[c, :, back], GA_Z + d, c)
+            arrive(ha.at[c, :, back], GA_Z[d], c)
             if c in DIRECT_GATHER:
                 continue
             part = ha.at[c, d, back]
-            remote(part, part, GA_F + d, c, dev_z[d]).start()
+            remote(part, part, GA_F, c, dev_z[d]).start()
 
     def step_6(c):
-        for d in range(2):
-            arrive(ha.at[c, d, z2], GA_F + d, c)
+        arrive(ha.at[c, :, z2], GA_F, c)
         arrive(hb.at[c, other], GB_Y, c)
         if once("down"):
             d_load.wait()
@@ -402,50 +383,35 @@
     def sent(ref, sem):
         pltpu.make_async_copy(ref, ref, sem).wait()
 
-    for d in range(2):
-        sent(pt_a.at[:, d], ssem.at[A_PT + d])
-        sent(pl_a.at[:, d], ssem.at[A_PL + d])
-        sent(cr_a.at[:, d], ssem.at[A_CB + d])
-        sent(pt_b.at[:, d], ssem.at[B_PT + d])
-        sent(pl_b.at[:, d], ssem.at[B_PL + d])
-        sent(cr_b.at[:, d], ssem.at[B_CB + d])
-        sent(ha.at[:, :, 0], ssem.at[GA_Z + d])
-        sent(ha.at[:, 0, 0], ssem.at[GA_F + d])
-        sent(hb.at[:, 0, 0], ssem.at[GB_Z + d])
-        sent(hb.at[:, 0, 0, :, pl.ds(0, HB2)], ssem.at[GB_F + d])
-    sent(yr_a, ssem.at[A_Y])
-    sent(yr_b, ssem.at[B_Y])
-    sent(ha.at[:, 0, 0], ssem.at[GA_Y])
-    sent(hb.at[:, 0], ssem.at[GB_Y])
-    sent(o2r, ssem.at[T_C])
-    sent(xr.at[pl.ds(2, NC - 2)], ssem.at[T_X])
-    sent(xs_all.at[:, pl.ds(0, ROWS)], ssem.at[X_CORE])
-    sent(xs_all.at[pl.ds(1, NC - 1), pl.ds(0, ROWS)], ssem.at[X_IN])
+    sent(pt_a, ssem.at[A_PT[0]])
+    sent(pc_a.at[:, 0], ssem.at[A_PL[0]])
+    sent(pc_a.at[:, 1], ssem.at[A_CB[0]])
+    sent(pt_b, ssem.at[B_PT[0]])
+    sent(pc_b.at[:, 0], ssem.at[B_PL[0]])
+    sent(pc_b.at[:, 1], ssem.at[B_CB[0]])
+    sent(ha.at[:, :, pl.ds(0, 2)], ssem.at[GA_Z[0][0]])
+    sent(ha.at[:, :, 0], ssem.at[GA_F[0]])
+    sent(hb.at[:, 0, pl.ds(0, 2)], ssem.at[GB_Z[0][0]])
+    sent(hb.at[:, 0, 0], ssem.at[GB_F[0]])
+    sent(yr_a, ssem.at[A_Y[0]])
+    sent(yr_b, ssem.at[B_Y[0]])
+    sent(ha.at[:, 0, 0], ssem.at[GA_Y[0]])
+    sent(hb.at[:, 0], ssem.at[GB_Y[0]])
+    sent(o2r, ssem.at[T_C[0]])
+    sent(xr.at[pl.ds(2, NC - 2)], ssem.at[T_X[0]])
+    sent(xs_all.at[:, pl.ds(0, ROWS)], ssem.at[X_CORE[0]])
+    sent(xs_all.at[pl.ds(1, NC - 1), pl.ds(0, ROWS)], ssem.at[X_IN[0]])
     yl_copy().wait_send()
 
-    def wait_sent(k, carry):
-        peer = (t + k) % 16
-        place_copy(k, peer).wait_send()
-        return carry
-
-    lax.fori_loop(1, 16, wait_sent, 0)
-
-    def wait_rows(k, carry):
-        row_arrive(k)
-        return carry
-
-    lax.fori_loop(1, 16, wait_rows, 0)
+    all_peers(pos_s, psend)
+    all_peers(got, grecv)
     for part in range(2):
         out = lax.dot_general(
             pick_r[part], got[...], (((0,), (0,)), ((), ())), preferred_element_type=F32
         )
         out_ref[:, part * half : (part + 1) * half] = out.astype(BF16)
 
-    def wait_rows_sent(k, carry):
-        row_copy(k, (t + k) % 16).wait_send()
-        return carry
-
-    lax.fori_loop(1, 16, wait_rows_sent, 0)
+    all_peers(snd, gsend)
 
 
 def local(doc_rows, packed_slot, gate_weight, up_weight, down_weight):
@@ -468,16 +434,14 @@
             buf(NC, 2, 2, 4, 16, CA),
             buf(NC, 2, 2, 4, 16, CB),
             buf(NC, 2, 2, 16, CA),
-            buf(NC, 2, 2, 16, CA),
-            buf(NC, 2, 2, 16, CA),
+            buf(NC, 2, 2, 2, 16, CA),
             buf(NC, 2, 2, 16, CA),
             buf(NC, 2, 16, CA),
             buf(NC, 2, 16, CA),
             buf(NC, 2, 4, 16, CB),
             buf(NC, 2, 4, 16, CB),
             buf(NC, 2, 16, CB),
-            buf(NC, 2, 16, CB),
-            buf(NC, 2, 16, CB),
+            buf(NC, 2, 2, 16, CB),
             buf(NC, 2, 16, CB),
             buf(NC, 2, 4, 16, CA),
             buf(NC, 2, 4, 16, CB),
@@ -494,17 +458,17 @@
             buf(256, 128, dtype=jnp.int32),
             buf(2, 256, ROWS),
             buf(2, 256, ROWS),
-            dma((2, TA + TB)),
+            dma((TA + TB,)),
             dma,
             dma,
             dma((KINDS,)),
             dma((KINDS, NC)),
             dma,
             dma,
-            dma((15,)),
-            dma((15,)),
-            dma((15,)),
-            dma((15,)),
+            dma,
+            dma,
+            dma,
+            dma,
         ],
         compiler_params=pltpu.CompilerParams(
             collective_id=0, has_side_effects=True, vmem_limit_bytes=60 << 20

time: 104 us -> 102 us (0.981)
  Pallas kernels: 103 us -> 100 us
    pallas_call x1, Pallas kernels: 103 us -> 100 us  [local(): pl.pallas_call(kernel, out_shape=jax.ShapeDtypeStruct((ROWS, WIDTH), BF16...]
where the time goes in v4:
time: 102 us
  Pallas kernels  100 us (98%)
  local copies, waits for them, and re-layouts  1.57 us (2%)
    pallas_call x1, Pallas kernels, local(): pl.pallas_call(kernel, out_shape=jax.ShapeDtypeStruct((ROWS, WIDTH), BF16...  100 us

profile of v4, /device:TPU:1, one launch (start us, length us, event | category | flops | bytes accessed | tf_op | source)
XLA Modules:
  0.0 102.0 jit_solution(3550393289309619756)
XLA Ops:
  0.0 100.4 %layer.1 = bf16[64,1024]{1,0:T(8,128)(2,1)} custom-call(s32[1,64]{1,0:T(1,128)} %bitcast.1, bf16[64,1024]{1,0:T(8,128)(2,1)} %doc_ref.1, bf16[1024,1792]{1,0:T(8,128)(2,1)} %gate_ref.1, bf16[1024,1792]{1,0:T(8,128)(2,1)} %up_ref.1, bf16[1792,1024]{1,0:T(8,128)(2,1)} %down_ref.1), custom_call_target="tpu_custom_call" | custom-call | flops 11274289152 | bytes 12582912 | tf_op jit(solution)/shard_map/layer/pallas_call | solution.py:425
  100.4 1.6 %copy.7 = bf16[64,1024]{1,0:T(8,128)(2,1)} copy(bf16[64,1024]{1,0:T(8,128)(2,1)} %layer.1) | data formatting | bytes 262144

commit v5 on v4

--- a/solution.py
+++ b/solution.py
@@ -471,7 +471,7 @@
             dma,
         ],
         compiler_params=pltpu.CompilerParams(
-            collective_id=0, has_side_effects=True, vmem_limit_bytes=60 << 20
+            collective_id=0, has_side_effects=True, vmem_limit_bytes=55040 << 10
         ),
         cost_estimate=pl.CostEstimate(
             flops=2 * 1024 * 1024 * 5376, bytes_accessed=12 << 20, transcendentals=1024 * 1792 // 8

time: 102 us -> 101 us (level)
    pallas_call x1, Pallas kernels: 100 us -> 99.1 us  [local(): pl.pallas_call(kernel, out_shape=jax.ShapeDtypeStruct((ROWS, WIDTH), BF16...]
where the time goes in v5:
time: 101 us; the launch traced here: 100 us
  Pallas kernels  99.1 us (98%)
  local copies, waits for them, and re-layouts  1.31 us (1%)
    pallas_call x1, Pallas kernels, local(): pl.pallas_call(kernel, out_shape=jax.ShapeDtypeStruct((ROWS, WIDTH), BF16...  99.1 us

profile of v5, /device:TPU:1, one launch (start us, length us, event | category | flops | bytes accessed | tf_op | source)
XLA Modules:
  0.0 100.4 jit_solution(7831364148048443904)
XLA Ops:
  0.0 0.0 copy-start
  0.0 0.7 copy-done
  0.7 99.1 %layer.1 = bf16[64,1024]{1,0:T(8,128)(2,1)S(1)} custom-call(s32[1,64]{1,0:T(1,128)S(1)} %bitcast.1, bf16[64,1024]{1,0:T(8,128)(2,1)} %doc_ref.1, bf16[1024,1792]{1,0:T(8,128)(2,1)} %gate_ref.1, bf16[1024,1792]{1,0:T(8,128)(2,1)} %up_ref.1, bf16[1792,1024]{1,0:T(8,128)(2,1)} %down_ref.1), custom_call_target="tpu_custom_call" | custom-call | flops 11274289152 | bytes 12582912 | tf_op jit(solution)/shard_map/layer/pallas_call | solution.py:425
  99.8 0.7 copy.7
Async XLA Ops:
  0.0 0.7 copy-start

commit v6 on v5

--- a/solution.py
+++ b/solution.py
@@ -22,8 +22,7 @@
 A_PT, A_PL, A_CB, A_Y, B_Y, B_PT, B_PL, B_CB = (0, 0), (1, 1), (2, 1), (3, 2), (4, 3), (5, 4), (6, 5), (7, 5)
 GA_Y, GA_F, GB_F, GB_Y = (8, 6), (9, 7), (10, 8), (11, 9)
 T_C, T_X, X_IN, X_CORE = (12, 10), (13, 11), (14, 12), (15, 13)
-GA_Z = ((16, 14), (16, 15))
-GB_Z = ((17, 16), (17, 17))
+GA_Z, GB_Z = (16, 14), (17, 15)
 KINDS = 18
 
 
@@ -150,10 +149,11 @@
 
     def take_places():
         all_peers(pos_g, precv)
-        q = lax.broadcasted_iota(jnp.int32, (256, ROWS), 0)
-        here = pos_g[:, 0:ROWS] == lax.broadcasted_iota(jnp.int32, (256, ROWS), 1)
+        q = lax.broadcasted_iota(jnp.int32, (256, 128), 0)
+        here = pos_g[...] == lax.broadcasted_iota(jnp.int32, (256, 128), 1)
         for half in range(2):
-            pick_r[half] = jnp.where(here & ((q // 8) % 2 == half), 1.0, 0.0).astype(BF16)
+            pick = jnp.where(here & ((q // 8) % 2 == half), 1.0, 0.0)
+            pick_r[half] = pick.T[0:ROWS].astype(BF16)
 
     def place_copy(k, peer):
         return pltpu.make_async_remote_copy(
@@ -268,7 +268,7 @@
         )
         hb[c, yh, z] = gated(g, u)
         for d in range(2):
-            remote(hb.at[c, yh, z], hb.at[c, yh, z], GB_Z[d], c, dev_z[d]).start()
+            remote(hb.at[c, yh, z], hb.at[c, yh, z], GB_Z, c, dev_z[d]).start()
         if c in DIRECT_GATHER:
             for d in range(2):
                 part = hb.at[c, yh, z, :, pl.ds(d * HB2, HB2)]
@@ -283,7 +283,8 @@
     def step_4b(c):
         for d in range(2):
             back = (zb, zn)[d]
-            arrive(hb.at[c, yh, back], GB_Z[d], c)
+            if d == 0:
+                arrive(hb.at[c, yh, pl.ds(0, 2)], GB_Z, c)
             if c in DIRECT_GATHER:
                 continue
             part = hb.at[c, yh, back, :, pl.ds(d * HB2, HB2)]
@@ -292,7 +293,7 @@
     def step_4a(c):
         arrive(ha.at[c, other, z], GA_Y, c)
         for d in range(2):
-            remote(ha.at[c, :, z], ha.at[c, :, z], GA_Z[d], c, dev_z[d]).start()
+            remote(ha.at[c, :, z], ha.at[c, :, z], GA_Z, c, dev_z[d]).start()
         if c in DIRECT_GATHER:
             for d in range(2):
                 remote(ha.at[c, d, z], ha.at[c, d, z], GA_F, c, dev_z2).start()
@@ -304,7 +305,8 @@
     def step_5a(c):
         for d in range(2):
             back = (zb, zn)[d]
-            arrive(ha.at[c, :, back], GA_Z[d], c)
+            if d == 0:
+                arrive(ha.at[c, :, pl.ds(0, 2)], GA_Z, c)
             if c in DIRECT_GATHER:
                 continue
             part = ha.at[c, d, back]
@@ -389,9 +391,9 @@
     sent(pt_b, ssem.at[B_PT[0]])
     sent(pc_b.at[:, 0], ssem.at[B_PL[0]])
     sent(pc_b.at[:, 1], ssem.at[B_CB[0]])
-    sent(ha.at[:, :, pl.ds(0, 2)], ssem.at[GA_Z[0][0]])
+    sent(ha.at[:, :, pl.ds(0, 2)], ssem.at[GA_Z[0]])
     sent(ha.at[:, :, 0], ssem.at[GA_F[0]])
-    sent(hb.at[:, 0, pl.ds(0, 2)], ssem.at[GB_Z[0][0]])
+    sent(hb.at[:, 0, pl.ds(0, 2)], ssem.at[GB_Z[0]])
     sent(hb.at[:, 0, 0], ssem.at[GB_F[0]])
     sent(yr_a, ssem.at[A_Y[0]])
     sent(yr_b, ssem.at[B_Y[0]])
@@ -406,9 +408,7 @@
     all_peers(pos_s, psend)
     all_peers(got, grecv)
     for part in range(2):
-        out = lax.dot_general(
-            pick_r[part], got[...], (((0,), (0,)), ((), ())), preferred_element_type=F32
-        )
+        out = jnp.dot(pick_r[part], got[...], preferred_element_type=F32)
         out_ref[:, part * half : (part + 1) * half] = out.astype(BF16)
 
     all_peers(snd, gsend)
@@ -457,12 +457,12 @@
             buf(256, 128, dtype=jnp.int32),
             buf(256, 128, dtype=jnp.int32),
             buf(2, 256, ROWS),
-            buf(2, 256, ROWS),
+            buf(2, ROWS, 256),
             dma((TA + TB,)),
             dma,
             dma,
             dma((KINDS,)),
-            dma((KINDS, NC)),
+            dma((16, NC)),
             dma,
             dma,
             dma,

time: 101 us -> 101 us (level)
  no operation moved by 1% of the time
where the time goes in v6:
time: 101 us
  Pallas kernels  99.8 us (99%)
  local copies, waits for them, and re-layouts  1.31 us (1%)
    pallas_call x1, Pallas kernels, local(): pl.pallas_call(kernel, out_shape=jax.ShapeDtypeStruct((ROWS, WIDTH), BF16...  99.8 us

profile of v6, /device:TPU:1, one launch (start us, length us, event | category | flops | bytes accessed | tf_op | source)
XLA Modules:
  0.0 101.1 jit_solution(5905128381190025965)
XLA Ops:
  0.0 0.0 copy-start
  0.0 0.7 copy-done
  0.7 99.8 %layer.1 = bf16[64,1024]{1,0:T(8,128)(2,1)S(1)} custom-call(s32[1,64]{1,0:T(1,128)S(1)} %bitcast.1, bf16[64,1024]{1,0:T(8,128)(2,1)} %doc_ref.1, bf16[1024,1792]{1,0:T(8,128)(2,1)} %gate_ref.1, bf16[1024,1792]{1,0:T(8,128)(2,1)} %up_ref.1, bf16[1792,1024]{1,0:T(8,128)(2,1)} %down_ref.1), custom_call_target="tpu_custom_call" | custom-call | flops 11274289152 | bytes 12582912 | tf_op jit(solution)/shard_map/layer/pallas_call | solution.py:425
  100.5 0.7 copy.7
Async XLA Ops:
  0.0 0.7 copy-start
